TPU v7x, 256 devices: a whole 4x4x8 slice. The times are simulated.
256 devices in a mesh: arc: 2 (over core), row: 8 (over x, z_hi), col: 16 (over y, z_lo).
Axes of the slice: x: 4, y: 4, z: 8 (z_hi: 2, z_lo: 4; z = z_hi * 4 + z_lo), core: 2. Of those that a mesh axis runs over, the one named last changes fastest.
Arguments:
- design: bfloat16 [24576, 6, 16, 64], P(('arc', 'row'), None, 'col'), may hold values from -0.03827328 to 0.03827328
- obs_weight: float32 [24576], P(('arc', 'row')), may hold values from 0.25 to 4
- prior: float32 [6, 16, 64], P(None, 'col'), may hold values from 0.3 to 3
Outputs:
- normal: float32 [12, 8, 64, 6, 16, 64], P(None, 'row', None, None, 'col')
- panel: float32 [12, 8, 64, 1024], P(None, 'row')
All inputs are finite; a program needn't handle non-finite values.
Results may differ from a plain program's by a relative error of at most 0.0012.
Values may be sent and summed in bfloat16 or wider, within the bound.
A program may use at most 128 MiB of HBM per device.

v0:
```python
import jax
import jax.numpy as jnp
from jax import lax
from jax.sharding import PartitionSpec as P


def body(design, obs_weight, prior):
    n_row = lax.axis_size("row")
    n_col = lax.axis_size("col")
    rows_dev, kc_tiles, single, tile = design.shape
    coeffs = kc_tiles * n_col * tile
    kt_rows = coeffs // tile // n_row
    local_cols = kc_tiles * tile
    weighted = (design.astype(jnp.float32) * obs_weight[:, None, None, None]).astype(jnp.bfloat16)
    weighted = weighted.reshape(rows_dev, local_cols)
    partial_gram = jnp.einsum(
        "rkct,rj->kctj",
        lax.all_gather(design, "col", axis=2, tiled=True),
        weighted,
        preferred_element_type=jnp.float32,
    )
    blocks = partial_gram.reshape(kt_rows, n_row, tile, local_cols)
    owned = lax.psum_scatter(blocks, "row", scatter_dimension=1, tiled=True)
    tiles = lax.psum(owned, "arc").reshape(kt_rows, tile, local_cols)
    row_id = lax.axis_index("row")
    col_id = lax.axis_index("col")
    tile_rows = jnp.arange(kt_rows, dtype=jnp.int32) * n_row + row_id
    tile_cols = jnp.arange(kc_tiles, dtype=jnp.int32) * n_col + col_id
    same = (tile_rows[:, None] == tile_cols[None, :]).astype(jnp.float32)
    identity = jnp.eye(tile, dtype=jnp.float32)
    added = (
        same[:, None, :, None]
        * identity[None, :, None, :]
        * prior.reshape(kc_tiles, tile)[None, None, :, :]
    )
    normal_tiles = tiles.reshape(kt_rows, tile, kc_tiles, tile) + added
    normal = normal_tiles.reshape(kt_rows, 1, tile, kc_tiles, 1, tile)
    leading = normal_tiles[:, :, 0, :].reshape(kt_rows * tile, tile)
    panel_rows = lax.all_gather(leading, "col", axis=1, tiled=True)
    width = panel_rows.shape[1]
    lead_tiles = width // (tile * n_row)
    top = panel_rows.reshape(kt_rows, 1, tile, width)[:lead_tiles]
    square = lax.all_gather(top, "row", axis=1, tiled=True).reshape(width, width)
    factor = jnp.linalg.cholesky(square)
    result = lax.linalg.triangular_solve(
        factor, panel_rows, left_side=False, lower=True, transpose_a=True
    )
    return (normal, result.reshape(kt_rows, 1, tile, width))


def solution(mesh):
    placed = (P(("arc", "row"), None, "col", None), P(("arc", "row")), P(None, "col", None))
    return jax.shard_map(
        body,
        mesh=mesh,
        in_specs=placed,
        out_specs=(P(None, "row", None, None, "col", None), P(None, "row", None, None)),
        check_vma=False,
    )
```

profile of v0, /device:TPU:105, one launch (start us, length us, event | category | flops | bytes accessed | tf_op | source)
XLA Modules:
  0.0 1233.1 jit_solution(4564662382012614200)
XLA Ops:
  7.9 1.5 multiply_convert_fusion
  9.4 397.7 %all-gather.4.cloned.1.call-done = bf16[1536,6,16,64]{0,3,2,1:T(8,128)(2,1)} async-done(((bf16[1536,6,1,64]{0,3,2,1:T(8,128)(2,1)}), bf16[1536,6,16,64]{0,3,2,1:T(8,128)(2,1)}) %all-gather.4.cloned.1.call-update) | async-done | bytes 18874384 | tf_op jit(solution)/shard_map/all_gather | solution.py:18
  407.1 13.2 %fusion.68 = f32[384,6144]{0,1:S(1)} fusion(bf16[1536,384]{0,1:T(8,128)(2,1)S(1)} %bitcast.134, bf16[1536,6144]{0,1:T(8,128)(2,1)} %bitcast.138), kind=kOutput, calls=%fused_computation.166 | convolution fusion | flops 7247757312 | bytes 29491200
  420.3 4.3 copy.26
  424.7 198.8 %reduce-scatter.2.cloned.1.call-done = f32[12,1,64,384]{3,2,0,1:T(8,128)} async-done(((f32[12,8,64,384]{3,2,0,1:T(8,128)}), f32[12,1,64,384]{3,2,0,1:T(8,128)}) %reduce-scatter.2.cloned.1.call-update) | async-done | bytes 1179664 | tf_op jit(solution)/shard_map/reduce_scatter | solution.py:23
  623.7 33.2 %all-reduce.3.cloned.1.call-done = f32[12,1,64,384]{3,2,0,1:T(8,128)} async-done(((f32[12,1,64,384]{3,2,0,1:T(8,128)}), f32[12,1,64,384]{3,2,0,1:T(8,128)}) %all-reduce.3.cloned.1.call-update) | async-done | bytes 1179664 | tf_op jit(solution)/shard_map/psum | solution.py:24
  656.9 3.2 reshape_reshape.6
  660.2 2.4 slice_add_fusion
  663.5 76.3 %all-gather.6.cloned.1.call-done = f32[768,1024]{0,1:T(8,128)} async-done(((f32[768,64]{0,1:T(8,128)}), f32[768,1024]{0,1:T(8,128)}) %all-gather.6.cloned.1.call-update) | async-done | bytes 3145744 | tf_op jit(solution)/shard_map/all_gather | solution.py:39
  739.8 1.1 slice.249
  742.0 2.7 reshape_reshape.5
  744.7 4.8 multiply_add_fusion
  755.5 103.3 %all-gather.8.cloned.1.call-done = f32[2,8,64,1024]{3,2,0,1:T(8,128)} async-done(((f32[2,1,64,1024]{3,2,0,1:T(8,128)}), f32[2,8,64,1024]{3,2,0,1:T(8,128)}) %all-gather.8.cloned.1.call-update) | async-done | bytes 4194320 | tf_op jit(solution)/shard_map/all_gather | solution.py:43
  858.8 4.7 copy.29
  863.5 5.8 copy.30
  869.3 4.4 fusion
  873.8 1.9 copy-done
  875.7 11.7 cholesky.223
  887.4 9.8 custom-call.62
  897.3 2.5 cholesky.255
  899.7 2.4 constant_dynamic-update-slice_fusion.32
  902.1 1.5 convolution_subtract_fusion
  903.7 11.9 cholesky.244
  916.2 9.8 custom-call.63
  926.0 1.2 convolution_dynamic-update-slice_fusion.1
  927.3 2.1 convolution_subtract_fusion.7
  929.4 11.7 cholesky.468
  942.4 9.8 custom-call.64
  952.2 1.2 convolution_dynamic-update-slice_fusion.2
  953.4 2.3 convolution_subtract_fusion.8
  955.8 11.9 cholesky.487
  969.0 9.8 custom-call.65
  978.8 1.1 convolution_dynamic-update-slice_fusion.3
  979.9 2.3 convolution_subtract_fusion.9
  982.3 11.7 cholesky.506
  995.3 10.2 custom-call.66
  1006.5 2.3 convolution_subtract_fusion.10
  1008.8 11.7 cholesky.526
  1021.9 9.8 custom-call.67
  1032.6 2.0 convolution_subtract_fusion.11
  1034.7 11.9 cholesky.546
  1047.9 9.8 custom-call.68
  1058.5 1.8 convolution_subtract_fusion.12
  1060.3 11.7 cholesky.564
  1079.2 4.8 select_select_fusion
  1084.0 27.8 %while.1 = (s32[]{:T(128)}, f32[1024,1024]{1,0:T(8,128)}, s32[8,2]{0,1:T(2,128)S(1)}, f32[8,128,128]{2,1,0:T(8,128)}, s32[]{:T(128)}) while((s32[]{:T(128)}, f32[1024,1024]{1,0:T(8,128)}, s32[8,2]{0,1:T(2,128)S(1)}, f32[8,128,128]{2,1,0:T(8,128)}, s32[]{:T(128)}) %tuple.71), condition=%wide.while_cond, body=%wide.while_body.sunk | while | flops 2 | bytes 132705 | solution.py:45
  1084.6 2.9 bitcast_dynamic-update-slice_fusion.2
  1088.1 2.9 bitcast_dynamic-update-slice_fusion.2
  1091.5 2.9 bitcast_dynamic-update-slice_fusion.2
  1095.0 2.9 bitcast_dynamic-update-slice_fusion.2
  1098.5 2.9 bitcast_dynamic-update-slice_fusion.2
  1102.0 2.9 bitcast_dynamic-update-slice_fusion.2
  1105.5 2.9 bitcast_dynamic-update-slice_fusion.2
  1108.9 2.8 bitcast_dynamic-update-slice_fusion.2
  1111.7 80.2 %custom-call.69 = f32[8,128,128]{1,2,0:T(8,128)} custom-call(f32[8,128,128]{2,1,0:T(8,128)} %get-tuple-element.9), custom_call_target="InvertDiagBlocksLowerTriangular" | custom-call | tf_op jit(solution)/shard_map/triangular_solve | solution.py:45
  1192.0 1.6 constant_dynamic-update-slice_fusion.17
  1193.7 1.8 convolution_subtract_fusion.4
  1196.1 2.5 convolution_subtract_fusion.6
  1199.2 3.0 convolution_subtract_fusion.3
  1202.9 3.7 fusion.9
  1207.1 4.6 convolution_subtract_fusion.2
  1212.2 4.9 convolution_subtract_fusion.5
  1217.7 5.6 convolution_subtract_fusion.1
  1223.8 2.4 copy.38
  (96 shorter events, 29.7 us)
Async XLA Ops:
  7.2 399.9 %all-gather.4.cloned.1.call-start = ((), (), s32[]{:S(2)}) async-start(), calls=%async_computation.1 | async-start | bytes 20054016 | tf_op jit(solution)/shard_map/all_gather | solution.py:18
  7.9 615.6 %reduce-scatter.2.cloned.1.call-start = ((), (), s32[]{:S(2)}) async-start(), calls=%async_computation.2 | async-start | bytes 10616832 | tf_op jit(solution)/shard_map/reduce_scatter | solution.py:23
  424.6 198.9 %copy-start.9 = (f32[6,1,64]{2,1,0:T(1,128)S(1)}, f32[6,1,64]{2,1,0:T(1,128)}, u32[]{:S(2)}) copy-start(f32[6,1,64]{2,1,0:T(1,128)} %param.5) | copy-start | bytes 4612
  424.6 232.3 %all-reduce.3.cloned.1.call-start = ((), (), s32[]{:S(2)}) async-start(), calls=%async_computation.3 | async-start | bytes 2359296 | tf_op jit(solution)/shard_map/psum | solution.py:24
  623.5 116.4 %all-gather.6.cloned.1.call-start = ((), (), s32[]{:S(2)}) async-start(), calls=%async_computation.4 | async-start | bytes 3342336 | tf_op jit(solution)/shard_map/all_gather | solution.py:39
  623.6 39.9 %copy-start.8 = (f32[64,64]{1,0:T(8,128)}, f32[64,64]{1,0:T(8,128)S(1)}, u32[]{:S(2)}) copy-start(f32[64,64]{1,0:T(8,128)S(1)} %fusion.62) | copy-start | bytes 49156
  660.2 81.8 %copy-start.1 = (f32[12,1,64,384]{3,2,0,1:T(8,128)S(1)}, f32[12,1,64,384]{3,2,0,1:T(8,128)}, u32[]{:S(2)}) copy-start(f32[12,1,64,384]{3,2,0,1:T(8,128)} %all-reduce.3.cloned.1.call-done) | copy-start | bytes 3538948
  663.5 195.3 %all-gather.8.cloned.1.call-start = ((), (), s32[]{:S(2)}) async-start(), calls=%async_computation.5 | async-start | bytes 4718592 | tf_op jit(solution)/shard_map/all_gather | solution.py:43
  744.7 4.8 copy-start.2
  873.7 1.9 copy-start
  1192.0 3.5 copy-start.6
  1195.5 3.7 copy-start.4
  1198.6 4.2 copy-start.7
  1202.8 4.2 copy-start.3
  1211.7 6.0 copy-start.5
Sparse Core Ops, SparseCore 0:
  9.8 397.2 all-gather.3
  424.7 198.6 reduce-scatter.1
  626.2 30.6 all-reduce.2
  663.6 76.2 all-gather.5
  742.9 115.8 all-gather.7
where the time goes:
time: 1250 us; the launch traced here: 1230 us
  waiting for transfers between devices  810 us (65%)
  other arithmetic  271 us (22%)
  matrix products  67.9 us (5%)
  local copies, waits for them, and re-layouts  64.3 us (5%)
  between operations  19.9 us (2%)
    all_gather x1, waiting for transfers between devices, body(): lax.all_gather(design, 'col', axis=2, tiled=True)  398 us
    reduce_scatter x1, waiting for transfers between devices, body(): owned = lax.psum_scatter(blocks, 'row', scatter_dimension=1, tiled=True)  199 us
    another operation x30, other arithmetic, body(): factor = jnp.linalg.cholesky(square)  173 us
    all_gather x1, waiting for transfers between devices, body(): lax.all_gather(top, 'row', axis=1, tiled=True).reshape(width, width)  103 us
    another operation x3, other arithmetic, body(): lax.linalg.triangular_solve(factor, panel_rows, left_side=False, lower=Tr...  85 us
    all_gather x1, waiting for transfers between devices, body(): panel_rows = lax.all_gather(leading, 'col', axis=1, tiled=True)  76.3 us
    psum x1, waiting for transfers between devices, body(): tiles = lax.psum(owned, 'arc').reshape(kt_rows, tile, local_cols)  33.2 us
    another operation x15, matrix products, body(): lax.linalg.triangular_solve(factor, panel_rows, left_side=False, lower=Tr...  31.6 us
  transfers between devices with their start and end apart: 5, of which 5 were waited for; matrix products, arithmetic and copies ran while one was open for 1% of the time, Pallas kernels for 0%

commit v1 on v0

v1 whole, which is shorter than its diff:
```python
import functools

import jax
import jax.numpy as jnp
from jax import lax
from jax.experimental import pallas as pl
from jax.experimental.pallas import tpu as pltpu
from jax.sharding import PartitionSpec as P

F32 = jnp.float32
BF16 = jnp.bfloat16
MESH = pl.DeviceIdType.MESH
VMEM = pl.BlockSpec(memory_space=pltpu.VMEM)
HIGHEST = lax.Precision.HIGHEST


def place():
    arc = lax.axis_index("arc")
    row = lax.axis_index("row")
    col = lax.axis_index("col")
    return arc, row // 2, row % 2, col // 4, col % 4


def device(arc, x, zh, y, zl):
    return (arc, x * 2 + zh, y * 4 + zl)


def host(z1, z2):
    low, high = jnp.minimum(z1, z2), jnp.maximum(z1, z2)
    apart = jnp.where(high == 2, 2, jnp.where(high == 1, 0, jnp.where(low == 2, 3, low)))
    return jnp.where(z1 == z2, z1, apart)


def pick(values, at):
    out = jnp.int32(values[0])
    for k in range(1, len(values)):
        out = jnp.where(at == k, values[k], out)
    return out


def gram_kernel(at_ref, w_ref, out_ref, ya, za, yw, zw, part, dbuf, xbuf, total, fbuf,
                ysend, yrecv, zsend, zrecv, dsend, drecv, xsend, xrecv, fsend, frecv, osend, orecv):
    arc, x, zh, y, zl = place()
    size, obs = at_ref.shape
    half, piece = size // 2, size // 8
    even = zl % 2 == 0
    moved = (pick((1, 3, 0, 2), zl), pick((3, 0, 1, 0), zl))
    goes = (pick((2, 0, 3, 1), zl), pick((0, 2, 0, 0), zl))
    mate = device(1 - arc, x, zh, y, zl)

    def owner(block):
        kind, slot, k = block
        other = (y + k) % 4
        if kind == "own":
            y1, z1, y2, z2 = y, zl, other, zl
        elif kind == "rows":
            y1, z1, y2, z2 = y, moved[slot], other, zl
        else:
            y1, z1, y2, z2 = other, zl, y, moved[slot]
        r = (y1 % 2) * 4 + z1
        target = (arc, r, y2 * 4 + z2)
        own_r = x * 2 + zh
        mine = (r == own_r) & (y2 == y) & (z2 == zl)
        return target, y1 // 2, mine

    blocks = [("own", 0, k) for k in range(4)]
    for slot in range(2):
        blocks += [("rows", slot, k) for k in range(4)] + [("cols", slot, k) for k in range(4)]

    bar = pltpu.get_barrier_semaphore()

    def greet(target):
        pl.semaphore_signal(bar, inc=1, device_id=target, device_id_type=MESH)

    count = jnp.int32(3 + 3 + 1 + 1)
    for k in (1, 2, 3):
        greet(device(arc, x, zh, (y + k) % 4, zl))
        greet(device(arc, (x + k) % 4, zh, y, zl))
    greet(mate)
    greet(device(arc, x, zh, y, moved[0]))

    @pl.when(even)
    def _():
        greet(device(arc, x, zh, y, moved[1]))

    count = count + jnp.where(even, 0, 1)
    r_own = x * 2 + zh
    for upper in range(2):
        y1, z1 = r_own // 4 + 2 * upper, r_own % 4
        plane = host(z1, zl)
        yy = jnp.where(z1 == zl, y1, jnp.where(plane == zl, y1, y))
        for xx in range(4):
            for zz in range(2):
                same = (xx == x) & (zz == zh) & (yy == y) & (plane == zl)

                @pl.when(jnp.logical_not(same))
                def _():
                    greet(device(arc, xx, zz, yy, plane))

    for b, block in enumerate(blocks):
        away = jnp.where(owner(block)[2], 0, 1)
        count = count + (away if b < 12 else jnp.where(even, away, 0))
    pl.semaphore_wait(bar, count)

    ycopies = []
    for k in (1, 3, 2):
        c = pltpu.make_async_remote_copy(at_ref, ya.at[(4 - k) % 4], ysend.at[k], yrecv.at[(4 - k) % 4],
                                         device_id=device(arc, x, zh, (y + k) % 4, zl), device_id_type=MESH)
        ycopies.append(c)
    zcopies = [pltpu.make_async_remote_copy(at_ref, za.at[s], zsend.at[s], zrecv.at[s],
                                            device_id=device(arc, x, zh, y, goes[s]), device_id_type=MESH)
               for s in range(2)]
    zcopies[0].start()

    @pl.when(jnp.logical_not(even))
    def _():
        zcopies[1].start()

    for c in ycopies:
        c.start()

    weight = w_ref[...]

    def weigh(src, dst):
        def chunk(i, carry):
            at = pl.ds(pl.multiple_of(i * 32, 32), 32)
            dst[at, :] = (src[at, :].astype(F32) * weight).astype(BF16)
            return carry

        lax.fori_loop(0, size // 32, chunk, 0)

    def times(left, right, into):
        into[...] = lax.dot_general(left[...], right[...], (((1,), (1,)), ((), ())), preferred_element_type=F32)

    def trade(first, n):
        return pltpu.make_async_remote_copy(
            part.at[pl.ds(first, n), pl.ds(pl.multiple_of((1 - arc) * half, half), half)],
            dbuf.at[pl.ds(first, n)], dsend.at[first // 4], drecv.at[first // 4],
            device_id=mate, device_id_type=MESH)

    def spread(first, n, k):
        peer = (x + k) % 4
        return pltpu.make_async_remote_copy(
            part.at[pl.ds(first, n), pl.ds(pl.multiple_of(arc * half + peer * piece, 16), piece)],
            xbuf.at[(4 - k) % 4, pl.ds(first, n)], xsend.at[k, first // 4], xrecv.at[(4 - k) % 4, first // 4],
            device_id=device(arc, peer, zh, y, zl), device_id_type=MESH)

    def halves(first, n):
        trade(first, n).wait()
        rows = pl.ds(pl.multiple_of(arc * half, half), half)

        def add(b, carry):
            part[first + b, rows] = part[first + b, rows] + dbuf[first + b]
            return carry

        lax.fori_loop(0, n, add, 0)
        for k in (1, 3, 2):
            spread(first, n, k).start()

    def deliver(first, n):
        for k in (1, 3, 2):
            spread(first, n, k).wait()
        rows = pl.ds(pl.multiple_of(arc * half + x * piece, 16), piece)

        def add(b, carry):
            at = first + b
            total[at] = (part[at, rows] + xbuf[1, at]) + (xbuf[2, at] + xbuf[3, at])
            return carry

        lax.fori_loop(0, n, add, 0)
        for b in range(first, first + n):
            final(b, "start")

    def final(b, act):
        target, upper, mine = owner(blocks[b])
        dst = fbuf.at[upper, zh, x]
        sem = frecv.at[upper, zh, x]

        @pl.when(mine)
        def _():
            if act == "start":
                pltpu.make_async_copy(total.at[b], dst, sem).start()

        @pl.when(jnp.logical_not(mine))
        def _():
            c = pltpu.make_async_remote_copy(total.at[b], dst, fsend.at[b], sem, device_id=target, device_id_type=MESH)
            if act == "start":
                c.start()
            else:
                c.wait_send()

    ya[0] = at_ref[...]
    weigh(at_ref, yw.at[0])
    for k in (1, 3, 2):
        pltpu.make_async_remote_copy(at_ref, ya.at[k], ysend.at[k], yrecv.at[k], device_id=mate, device_id_type=MESH).wait_recv()
        weigh(ya.at[k], yw.at[k])

    def own_block(k, carry):
        times(at_ref, yw.at[k], part.at[k])
        return carry

    lax.fori_loop(0, 4, own_block, 0)
    trade(0, 4).start()

    def moved_blocks(s):
        zcopies[s].wait_recv()
        weigh(za.at[s], zw.at[s])

        def one(k, carry):
            times(za.at[s], yw.at[k], part.at[4 + 8 * s + k])
            times(ya.at[k], zw.at[s], part.at[8 + 8 * s + k])
            return carry

        lax.fori_loop(0, 4, one, 0)
        trade(4 + 8 * s, 8).start()

    moved_blocks(0)
    halves(0, 4)

    @pl.when(even)
    def _():
        moved_blocks(1)

    halves(4, 8)

    @pl.when(even)
    def _():
        halves(12, 8)

    deliver(0, 4)
    deliver(4, 8)

    @pl.when(even)
    def _():
        deliver(12, 8)

    for upper in range(2):
        for xx in range(4):
            for zz in range(2):
                pltpu.make_async_copy(total.at[0], fbuf.at[upper, zz, xx], frecv.at[upper, zz, xx]).wait()
            at = pl.ds(pl.multiple_of(arc * half + xx * piece, 16), piece)
            out_ref[upper, at] = fbuf[upper, 0, xx] + fbuf[upper, 1, xx]
    rows = pl.ds(pl.multiple_of(arc * half, half), half)
    back = pltpu.make_async_remote_copy(out_ref.at[:, rows], out_ref.at[:, rows], osend, orecv,
                                        device_id=mate, device_id_type=MESH)
    back.start()

    for c in ycopies:
        c.wait_send()
    zcopies[0].wait_send()

    @pl.when(jnp.logical_not(even))
    def _():
        zcopies[1].wait_send()

    for b in range(12):
        final(b, "end")

    @pl.when(even)
    def _():
        for b in range(12, 20):
            final(b, "end")

    back.wait()


def gram_block(at, weight):
    size, obs = at.shape
    dma = pltpu.SemaphoreType.DMA
    return pl.pallas_call(
        gram_kernel,
        out_shape=jax.ShapeDtypeStruct((2, size, size), F32),
        in_specs=[VMEM, VMEM],
        out_specs=VMEM,
        scratch_shapes=[
            pltpu.VMEM((4, size, obs), BF16),
            pltpu.VMEM((2, size, obs), BF16),
            pltpu.VMEM((4, size, obs), BF16),
            pltpu.VMEM((2, size, obs), BF16),
            pltpu.VMEM((20, size, size), F32),
            pltpu.VMEM((20, size // 2, size), F32),
            pltpu.VMEM((4, 20, size // 8, size), F32),
            pltpu.VMEM((20, size // 8, size), F32),
            pltpu.VMEM((2, 2, 4, size // 8, size), F32),
            dma((4,)), dma((4,)), dma((2,)), dma((2,)), dma((5,)), dma((5,)),
            dma((4, 5)), dma((4, 5)), dma((20,)), dma((2, 2, 4)), dma, dma,
        ],
        compiler_params=pltpu.CompilerParams(collective_id=0, has_side_effects=True, vmem_limit_bytes=58 << 20),
        name="gram_block",
    )(at, weight)


def factor_inverse(block):
    n = block.shape[0]
    lane = lax.broadcasted_iota(jnp.int32, (8, n), 1)
    sub = lax.broadcasted_iota(jnp.int32, (8, n), 0)
    groups = [block[8 * g : 8 * g + 8, :] for g in range(n // 8)]
    for q in range(n // 8):
        pivot = groups[q]
        inside = (lane >= 8 * q) & (lane < 8 * q + 8)
        cols = [jnp.broadcast_to(pivot[:, 8 * q + j : 8 * q + j + 1], (8, n)) for j in range(8)]
        rows = jnp.where(inside, (lane - 8 * q == sub).astype(F32), pivot)
        scale, mult, scaled = [], {}, []
        for j in range(8):
            r = lax.rsqrt(cols[j][j : j + 1, :])
            scale.append(r)
            m = jnp.where(sub > j, cols[j] * r, 0.0)
            for l in range(j + 1, 8):
                mult[j, l] = cols[l][j : j + 1, :] * r
                cols[l] = cols[l] - m * mult[j, l]
            top = rows[j : j + 1, :] * r
            scaled.append(top)
            rows = jnp.where(sub == j, top, rows - m * top)
        groups[q] = rows
        for g in range(q + 1, n // 8):
            low = groups[g]
            c = [jnp.broadcast_to(low[:, 8 * q + j : 8 * q + j + 1], (8, n)) for j in range(8)]
            low = jnp.where(inside, 0.0, low)
            for j in range(8):
                m = c[j] * scale[j]
                for l in range(j + 1, 8):
                    c[l] = c[l] - m * mult[j, l]
                low = low - m * scaled[j]
            groups[g] = low
    lane_all = lax.broadcasted_iota(jnp.int32, (n, n), 1)
    sub_all = lax.broadcasted_iota(jnp.int32, (n, n), 0)
    return jnp.where(lane_all <= sub_all, jnp.concatenate(groups, axis=0), 0.0)


def inverse_factor(v_ref):
    n, b = v_ref.shape[0], 128
    steps = n // b

    def step(p, carry):
        at = pl.ds(pl.multiple_of(p * b, b), b)
        inv = factor_inverse(v_ref[at, at])
        v_ref[at, at] = jnp.eye(b, dtype=F32)
        v_ref[at, :] = jnp.dot(inv, v_ref[at, :], precision=HIGHEST, preferred_element_type=F32)

        def below(i, carry):
            here = pl.ds(pl.multiple_of(i * b, b), b)
            left = v_ref[at, here]
            v_ref[here, at] = jnp.zeros((b, b), F32)
            v_ref[here, :] = v_ref[here, :] - lax.dot_general(
                left, v_ref[at, :], (((0,), (0,)), ((), ())), precision=HIGHEST, preferred_element_type=F32)
            return carry

        lax.fori_loop(p + 1, steps, below, 0)
        return carry

    lax.fori_loop(0, steps, step, 0)


def panel_kernel(lead_ref, out_ref, gt, g11, v, zs, zr, ys, yr, cs, cr, hs, hr, xs, xr, ms, mr):
    arc, x, zh, y, zl = place()
    col = y * 4 + zl
    row = x * 2 + zh
    mate = device(1 - arc, x, zh, y, zl)
    bar = pltpu.get_barrier_semaphore()

    def greet(target):
        pl.semaphore_signal(bar, inc=1, device_id=target, device_id_type=MESH)

    greet(mate)
    greet(device(arc, x, 1 - zh, y, zl))
    for k in (1, 2, 3):
        greet(device(arc, x, zh, y, (zl + k) % 4))
        greet(device(arc, x, zh, (y + k) % 4, zl))
        greet(device(arc, (x + k) % 4, zh, y, zl))
    pl.semaphore_wait(bar, 11)

    parts = (pl.ds(0, 128), pl.ds(128, 640))

    def along_z(p, k):
        to = (zl + k) % 4
        return pltpu.make_async_remote_copy(
            lead_ref.at[arc, :, parts[p]], gt.at[col, arc, :, parts[p]], zs.at[p, k], zr.at[p, (4 - k) % 4],
            device_id=device(arc, x, zh, y, to), device_id_type=MESH)

    def along_y(p, k):
        view = gt.at[pl.ds(y * 4, 4), arc, :, parts[p]]
        return pltpu.make_async_remote_copy(
            view, view, ys.at[p, k], yr.at[p, (4 - k) % 4],
            device_id=device(arc, x, zh, (y + k) % 4, zl), device_id_type=MESH)

    def across(p):
        view = gt.at[:, arc, :, parts[p]]
        return pltpu.make_async_remote_copy(view, view, cs.at[p], cr.at[p], device_id=mate, device_id_type=MESH)

    for p in range(2):
        for k in (1, 3, 2):
            along_z(p, k).start()
    gt[col, arc] = lead_ref[arc]
    for p in range(2):
        for k in (1, 3, 2):
            along_z(p, k).wait()
        for k in (1, 3, 2):
            along_y(p, k).start()
        if p == 0:
            for k in (1, 3, 2):
                along_y(p, k).wait()
            for c in range(16):
                g11[row, c, arc] = gt[c, arc, :, 0:128]
            view = g11.at[row, :, arc]
            hop = pltpu.make_async_remote_copy(view, view, hs, hr, device_id=device(arc, x, 1 - zh, y, zl), device_id_type=MESH)
            hop.start()
            hop.wait()
            view = g11.at[pl.ds(x * 2, 2), :, arc]
            hops = [pltpu.make_async_remote_copy(view, view, xs.at[k], xr.at[(4 - k) % 4],
                                                 device_id=device(arc, (x + k) % 4, zh, y, zl), device_id_type=MESH)
                    for k in (1, 3, 2)]
            for h in hops:
                h.start()
            for h in hops:
                h.wait()
            view = g11.at[:, :, arc]
            hop = pltpu.make_async_remote_copy(view, view, ms, mr, device_id=mate, device_id_type=MESH)
            hop.start()
            hop.wait()
            across(0).start()

    def assemble(c, carry):
        at = pl.ds(pl.multiple_of(c * 64, 64), 64)
        for j in range(8):
            lanes = pl.ds((j // 4) * 64, 64)
            first, second = 2 * (j % 4), 2 * (j % 4) + 1
            v[at, j * 128 : j * 128 + 128] = jnp.concatenate(
                [g11[first, c].reshape(64, 128)[:, (j // 4) * 64 : (j // 4) * 64 + 64],
                 g11[second, c].reshape(64, 128)[:, (j // 4) * 64 : (j // 4) * 64 + 64]], axis=1)
        return carry

    lax.fori_loop(0, 16, assemble, 0)

    def symmetric(i, carry):
        at = pl.ds(pl.multiple_of(i * 128, 128), 128)

        def one(j, carry):
            here = pl.ds(pl.multiple_of(j * 128, 128), 128)
            upper = v[at, here]
            mean = 0.5 * (upper + v[here, at].T)
            v[at, here] = mean
            v[here, at] = mean.T
            return carry

        return lax.fori_loop(i, 8, one, carry)

    lax.fori_loop(0, 8, symmetric, 0)
    inverse_factor(v)
    for j in range(4):
        v[j * 256 : j * 256 + 128, j * 256 + 128 : j * 256 + 256] = jnp.zeros((128, 128), F32)

    for k in (1, 3, 2):
        along_y(1, k).wait()
    across(1).start()
    for p in range(2):
        across(p).wait()

    def strip(j, carry):
        at = pl.ds(pl.multiple_of(j * 256, 256), 256)

        def one(k, total):
            here = pl.ds(pl.multiple_of(k * 256, 256), 256)
            rows = gt[pl.ds(k * 4, 4)].reshape(256, 768)
            return total + jnp.dot(v[at, here], rows, precision=HIGHEST, preferred_element_type=F32)

        total = lax.fori_loop(0, j + 1, one, jnp.zeros((256, 768), F32))
        out_ref[:, at] = total.T
        return carry

    lax.fori_loop(0, 4, strip, 0)


def panel_rows(lead):
    dma = pltpu.SemaphoreType.DMA
    width = lead.shape[-1]
    return pl.pallas_call(
        panel_kernel,
        out_shape=jax.ShapeDtypeStruct((width, 1024), F32),
        in_specs=[VMEM],
        out_specs=VMEM,
        scratch_shapes=[
            pltpu.VMEM((16, 2, 32, width), F32),
            pltpu.VMEM((8, 16, 2, 32, 128), F32),
            pltpu.VMEM((1024, 1024), F32),
            dma((2, 4)), dma((2, 4)), dma((2, 4)), dma((2, 4)), dma((2,)), dma((2,)), dma, dma, dma((4,)), dma((4,)), dma, dma,
        ],
        compiler_params=pltpu.CompilerParams(collective_id=1, has_side_effects=True, vmem_limit_bytes=58 << 20),
        name="panel_rows",
    )(lead)


def body(design, obs_weight, prior):
    rows_dev, kc_tiles, single, tile = design.shape
    n_row, n_col = lax.axis_size("row"), lax.axis_size("col")
    local_cols = kc_tiles * tile
    gram = gram_block(design.transpose(1, 2, 3, 0).reshape(local_cols, rows_dev), obs_weight.reshape(1, rows_dev))
    tiles = gram.reshape(2, kc_tiles, tile, kc_tiles, tile).transpose(1, 0, 2, 3, 4).reshape(2 * kc_tiles, tile, kc_tiles, tile)
    row_id = lax.axis_index("row")
    col_id = lax.axis_index("col")
    kt_rows = 2 * kc_tiles
    tile_rows = jnp.arange(kt_rows, dtype=jnp.int32) * n_row + row_id
    tile_cols = jnp.arange(kc_tiles, dtype=jnp.int32) * n_col + col_id
    same = (tile_rows[:, None] == tile_cols[None, :]).astype(F32)
    added = (same[:, None, :, None] * jnp.eye(tile, dtype=F32)[None, :, None, :]
             * prior.reshape(kc_tiles, tile)[None, None, :, :])
    normal = tiles + added
    lead = normal[:, :, 0, :].reshape(kt_rows * tile, tile).T.reshape(2, tile // 2, kt_rows * tile)
    panel = panel_rows(lead)
    return (normal.reshape(kt_rows, 1, tile, kc_tiles, 1, tile), panel.reshape(kt_rows, 1, tile, 1024))


def solution(mesh):
    placed = (P(("arc", "row"), None, "col", None), P(("arc", "row")), P(None, "col", None))
    return jax.shard_map(
        body,
        mesh=mesh,
        in_specs=placed,
        out_specs=(P(None, "row", None, None, "col", None), P(None, "row", None, None)),
        check_vma=False,
    )
```

time: 1250 us -> 333 us (0.27)
  waiting for transfers between devices: 810 us -> 0 us
  Pallas kernels: 0 us -> 313 us
  other arithmetic: 271 us -> 0.54 us
  matrix products: 67.9 us -> 0 us
  local copies, waits for them, and re-layouts: 64.3 us -> 13.2 us
  between operations: 19.9 us -> 0.69 us
    all_gather x3 -> x0, waiting for transfers between devices: 577 us -> none  [the longest x1 398 us: body(): lax.all_gather(design, 'col', axis=2, tiled=True)]
    pallas_call x0 -> x2, Pallas kernels: none -> 313 us  [the longest x1 176 us: gram_block(): pl.pallas_call(gram_kernel, out_shape=jax.ShapeDtypeStruct((2, size, size...]
    another operation x33 -> x0, other arithmetic: 258 us -> none  [the longest x30 173 us: body(): factor = jnp.linalg.cholesky(square)]
    reduce_scatter x1 -> x0, waiting for transfers between devices: 199 us -> none  [body(): owned = lax.psum_scatter(blocks, 'row', scatter_dimension=1, tiled=True)]
    another operation x29 -> x0, matrix products: 54.7 us -> none  [the longest x15 31.6 us: body(): lax.linalg.triangular_solve(factor, panel_rows, left_side=False, lower=Tr...]
    another operation x38 -> x1, local copies, waits for them, and re-layouts: 39.7 us -> 0.83 us  [body(): normal[:, :, 0, :].reshape(kt_rows * tile, tile)]
    psum x1 -> x0, waiting for transfers between devices: 33.2 us -> none  [body(): tiles = lax.psum(owned, 'arc').reshape(kt_rows, tile, local_cols)]
    unnamed x1 -> x0, matrix products: 13.2 us -> none
  transfers between devices with their start and end apart: 5 -> 0, of which waited for: 5 -> 0; matrix products, arithmetic and copies ran while one was open for 1% -> 0% of each run, Pallas kernels for 0% -> 0%
where the time goes in v1:
time: 333 us; the launch traced here: 328 us
  Pallas kernels  313 us (94%)
  local copies, waits for them, and re-layouts  13.2 us (4%)
    pallas_call x1, Pallas kernels, gram_block(): pl.pallas_call(gram_kernel, out_shape=jax.ShapeDtypeStruct((2, size, size...  176 us
    pallas_call x1, Pallas kernels, panel_rows(): pl.pallas_call(panel_kernel, out_shape=jax.ShapeDtypeStruct((width, 1024)...  137 us
    unnamed x3, local copies, waits for them, and re-layouts  8.49 us

profile of v1, /device:TPU:105, one launch (start us, length us, event | category | flops | bytes accessed | tf_op | source)
XLA Modules:
  0.0 327.8 jit_solution(8030581400615727645)
XLA Ops:
  0.7 0.7 copy.17
  1.4 1.3 reshape.88.w_ref
  2.6 0.1 compare_convert_fusion
  2.7 175.9 %gram_block.1 = f32[2,384,384]{2,1,0:T(8,128)} custom-call(bf16[384,1536]{1,0:T(8,128)(2,1)} %bitcast.22, f32[1,1536]{1,0:T(1,128)} %reshape.88.w_ref), custom_call_target="tpu_custom_call" | custom-call | tf_op jit(solution)/shard_map/gram_block/pallas_call | solution.py:270
  178.7 2.2 reshape.89
  180.9 0.4 copy.9
  181.3 0.1 slice_add_fusion
  181.4 0.3 multiply_add_fusion
  181.8 3.8 %copy.12 = f32[12,1,64,6,1,64]{5,4,3,2,1,0:T(1,128)} copy(f32[12,1,64,6,1,64]{5,2,4,3,1,0:T(8,128)S(1)} %multiply_add_fusion) | data formatting | bytes 2359296
  185.6 0.8 copy.14
  186.4 137.4 %panel_rows.1 = f32[768,1024]{1,0:T(8,128)} custom-call(f32[2,32,768]{2,1,0:T(8,128)} %bitcast.23), custom_call_target="tpu_custom_call" | custom-call | tf_op jit(solution)/shard_map/panel_rows/pallas_call | solution.py:476
  323.9 4.0 %copy.19 = f32[12,1,64,1024]{3,2,1,0:T(8,128)} copy(f32[12,1,64,1024]{3,2,1,0:T(8,128)} %bitcast.17) | data formatting | bytes 6291456
  (4 shorter events, 0.0 us)

commit v2 on v0

v2 whole, which is shorter than its diff:
```python
import functools

import jax
import jax.numpy as jnp
from jax import lax
from jax.experimental import pallas as pl
from jax.experimental.pallas import tpu as pltpu
from jax.sharding import PartitionSpec as P

F32 = jnp.float32
BF16 = jnp.bfloat16
MESH = pl.DeviceIdType.MESH
VMEM = pl.BlockSpec(memory_space=pltpu.VMEM)
HIGHEST = lax.Precision.HIGHEST


def place():
    arc = lax.axis_index("arc")
    row = lax.axis_index("row")
    col = lax.axis_index("col")
    return arc, row // 2, row % 2, col // 4, col % 4


def device(arc, x, zh, y, zl):
    return (arc, x * 2 + zh, y * 4 + zl)


def pick(values, at):
    out = jnp.int32(values[0])
    for k in range(1, len(values)):
        out = jnp.where(at == k, values[k], out)
    return out


def factor_inverse(block):
    n = block.shape[0]
    lane = lax.broadcasted_iota(jnp.int32, (8, n), 1)
    sub = lax.broadcasted_iota(jnp.int32, (8, n), 0)
    groups = [block[8 * g : 8 * g + 8, :] for g in range(n // 8)]
    for q in range(n // 8):
        pivot = groups[q]
        inside = (lane >= 8 * q) & (lane < 8 * q + 8)
        cols = [jnp.broadcast_to(pivot[:, 8 * q + j : 8 * q + j + 1], (8, n)) for j in range(8)]
        rows = jnp.where(inside, (lane - 8 * q == sub).astype(F32), pivot)
        scale, mult, scaled = [], {}, []
        for j in range(8):
            r = lax.rsqrt(cols[j][j : j + 1, :])
            scale.append(r)
            m = jnp.where(sub > j, cols[j] * r, 0.0)
            for l in range(j + 1, 8):
                mult[j, l] = cols[l][j : j + 1, :] * r
                cols[l] = cols[l] - m * mult[j, l]
            top = rows[j : j + 1, :] * r
            scaled.append(top)
            rows = jnp.where(sub == j, top, rows - m * top)
        groups[q] = rows
        for g in range(q + 1, n // 8):
            low = groups[g]
            c = [jnp.broadcast_to(low[:, 8 * q + j : 8 * q + j + 1], (8, n)) for j in range(8)]
            low = jnp.where(inside, 0.0, low)
            for j in range(8):
                m = c[j] * scale[j]
                for l in range(j + 1, 8):
                    c[l] = c[l] - m * mult[j, l]
                low = low - m * scaled[j]
            groups[g] = low
    lane_all = lax.broadcasted_iota(jnp.int32, (n, n), 1)
    sub_all = lax.broadcasted_iota(jnp.int32, (n, n), 0)
    return jnp.where(lane_all <= sub_all, jnp.concatenate(groups, axis=0), 0.0)


CHUNKS = ((0, 64), (64, 160), (224, 160))
GROUPS = ((0, 9), (9, 3), (12, 8))


def kernel(at_ref, w_ref, prior_ref, norm_ref, panel_ref, out_ref,
           ya, za, yw, zw, part, dbuf, narrow, xf, xb, fbuf, strip, sbuf, mine, sx, sz, seen, v, rcat, gt,
           ysend, yrecv, zsend, zrecv, dsend, drecv, fxs, fxr, bxs, bxr, fsend, frecv, osend, orecv,
           s1s, s1r, s2s, s2r, s3s, s3r, s4s, s4r, s5s, s5r, s6s, s6r, s7s, s7r, gzs, gzr, gys, gyr, gcs, gcr):
    arc, x, zh, y, zl = place()
    size, obs = at_ref.shape
    half, piece = size // 2, size // 8
    even = zl % 2 == 0
    odd = jnp.logical_not(even)
    moved = (pick((1, 3, 0, 2), zl), pick((3, 0, 1, 0), zl))
    goes = (pick((2, 0, 3, 1), zl), pick((0, 2, 0, 0), zl))
    mate = device(1 - arc, x, zh, y, zl)
    zpeer = device(arc, x, 1 - zh, y, zl)
    col, row = y * 4 + zl, x * 2 + zh
    turns = (1, 3, 2)

    def xpeer(k):
        return device(arc, (x + k) % 4, zh, y, zl)

    def ypeer(k):
        return device(arc, x, zh, (y + k) % 4, zl)

    def lpeer(k):
        return device(arc, x, zh, y, (zl + k) % 4)

    def back(at, k):
        return (at + 4 - k) % 4

    def remote(src, dst, send, recv, target):
        return pltpu.make_async_remote_copy(src, dst, send, recv, device_id=target, device_id_type=MESH)

    blocks = [(kind, 0, k) for kind in ("own", "rows", "cols") for k in (0, 1, 3)]
    blocks += [(kind, 0, 2) for kind in ("own", "rows", "cols")]
    blocks += [(kind, 1, k) for kind in ("rows", "cols") for k in range(4)]

    def owner(block):
        kind, slot, k = block
        k = (y + k) % 4
        if kind == "own":
            y1, z1, y2, z2 = y, zl, k, zl
        elif kind == "rows":
            y1, z1, y2, z2 = y, moved[slot], k, zl
        else:
            y1, z1, y2, z2 = k, zl, y, moved[slot]
        r = (y1 % 2) * 4 + z1
        here = (r == row) & (y2 == y) & (z2 == zl)
        return (arc, r, y2 * 4 + z2), y1 // 2, here

    bar = pltpu.get_barrier_semaphore()

    def greet(target):
        pl.semaphore_signal(bar, inc=1, device_id=target, device_id_type=MESH)

    for k in turns:
        greet(ypeer(k))
        greet(xpeer(k))
        greet(lpeer(k))
    greet(mate)
    greet(zpeer)
    pl.semaphore_wait(bar, 11)

    def ycopy(c, k):
        at = pl.ds(*CHUNKS[c])
        return remote(at_ref.at[at], ya.at[y, at], ysend.at[c, k], yrecv.at[c, k], ypeer(k))

    def yarrival(c, k):
        at = pl.ds(*CHUNKS[c])
        return remote(at_ref.at[at], ya.at[back(y, k), at], ysend.at[c, k], yrecv.at[c, k], ypeer(k))

    def zcopy(c, s):
        at = pl.ds(*CHUNKS[c])
        return remote(at_ref.at[at], za.at[s, at], zsend.at[c, s], zrecv.at[c, s], device(arc, x, zh, y, goes[s]))

    def send_z(c, s):
        if s == 0:
            zcopy(c, 0).start()
        else:
            @pl.when(odd)
            def _():
                zcopy(c, 1).start()

    def send_y(c, ks):
        for k in ks:
            ycopy(c, k).start()

    def weigh(src, dst, c):
        first, rows = CHUNKS[c]

        def chunk(i, carry):
            at = pl.ds(pl.multiple_of(first + i * 32, 32), 32)
            dst[at, :] = (src[at, :].astype(F32) * w_ref[...]).astype(BF16)
            return carry

        lax.fori_loop(0, rows // 32, chunk, 0)

    def take_z(c, s):
        def go():
            zcopy(c, s).wait_recv()
            weigh(za.at[s], zw.at[s], c)

        if s == 0:
            go()
        else:
            pl.when(even)(go)

    def take_y(c, ks):
        for k in ks:
            yarrival(c, k).wait_recv()
            weigh(ya.at[back(y, k)], yw.at[back(y, k)], c)

    near, far = (1, 3), (2,)
    send_z(0, 0)
    send_y(0, near)
    send_z(0, 1)
    send_y(0, far)
    ya[y] = at_ref[...]
    for c in range(len(CHUNKS)):
        weigh(at_ref, yw.at[y], c)

    def nt(a, b):
        return lax.dot_general(a, b, (((1,), (1,)), ((), ())), preferred_element_type=F32)

    take_z(0, 0)
    take_y(0, near)
    take_z(0, 1)
    take_y(0, far)
    send_z(1, 0)
    send_y(1, near)
    send_z(2, 0)
    send_y(2, near)
    ahead_w = yw[:, 0:64, :].reshape(256, obs)
    strip[0] = 0.5 * nt(at_ref[0:64, :], ahead_w)
    ahead_a = ya[:, 0:64, :].reshape(256, obs)
    strip[1] = 0.5 * (nt(za[0, 0:64, :], ahead_w) + nt(zw[0, 0:64, :], ahead_a))

    @pl.when(even)
    def _():
        strip[2] = 0.5 * (nt(za[1, 0:64, :], yw[:, 0:64, :].reshape(256, obs)) + nt(zw[1, 0:64, :], ya[:, 0:64, :].reshape(256, obs)))

    @pl.when(odd)
    def _():
        strip[2] = jnp.zeros((64, 256), F32)

    theirs = pl.ds(pl.multiple_of((1 - arc) * 32, 32), 32)
    ours = pl.ds(pl.multiple_of(arc * 32, 32), 32)
    s1 = remote(strip.at[:, theirs], sbuf, s1s, s1r, mate)
    s1.start()
    s1.wait()
    mine[...] = strip[:, ours] + sbuf[...]
    def share(k):
        return pl.ds(pl.multiple_of(((x + k) % 4) * 8, 8), 8)

    own = share(0)
    s2 = [remote(mine.at[:, share(k)], sx.at[x], s2s.at[k], s2r.at[k], xpeer(k)) for k in turns]
    for c in s2:
        c.start()
    sx[x] = mine[:, own]
    for c in s2:
        c.wait()
    sz[zh] = (sx[0] + sx[1]) + (sx[2] + sx[3])
    s3 = remote(sz.at[zh], sz.at[zh], s3s, s3r, zpeer)
    s3.start()
    s3.wait()
    sums = sz[0] + sz[1]
    lane = lax.broadcasted_iota(jnp.int32, (8, 256), 1)
    sub = lax.broadcasted_iota(jnp.int32, (8, 256), 0)
    prior4 = jnp.concatenate([prior_ref[0]] * 4, axis=1)
    diagonal = jnp.where(lane == y * 64 + arc * 32 + x * 8 + sub, 0.5 * prior4, 0.0)
    seen[arc, y, zl, 0, own] = sums[0] + diagonal
    seen[arc, y, zl, 1, own] = sums[1]
    seen[arc, y, zl, 2, own] = sums[2]
    view = seen.at[arc, y, zl, :, own]
    s4 = [remote(view, view, s4s.at[k], s4r.at[k], lpeer(k)) for k in turns]
    for c in s4:
        c.start()
    for c in s4:
        c.wait()
    low, high = pl.ds(0, 2), pl.ds(2, 2)

    def both_ways(first, second, send, recv):
        return ([remote(first, first, send.at[0, k], recv.at[0, k], xpeer(k)) for k in turns]
                + [remote(second, second, send.at[1, k], recv.at[1, k], ypeer(k)) for k in turns])

    s5 = both_ways(seen.at[arc, y, low, :, own], seen.at[arc, y, high, :, own], s5s, s5r)
    for c in s5:
        c.start()
    for c in s5:
        c.wait()
    s6 = both_ways(seen.at[arc, :, high, :, own], seen.at[arc, y, low], s6s, s6r)
    for c in s6:
        c.start()
    send_z(1, 1)
    send_y(1, far)
    send_z(2, 1)
    send_y(2, far)
    s7 = remote(seen.at[arc], seen.at[arc], s7s, s7r, mate)

    def trade(g):
        first, n = GROUPS[g]
        return remote(part.at[pl.ds(first, n), pl.ds(pl.multiple_of((1 - arc) * half, half), half)],
                      dbuf.at[pl.ds(first, n)], dsend.at[g], drecv.at[g], mate)

    def products(first, n, kind, slot, shift):
        def one(i, carry):
            k = (y + shift(i)) % 4
            if kind == "own":
                part[first + i] = nt(at_ref[...], yw[k])
            elif kind == "rows":
                part[first + i] = nt(za[slot], yw[k])
            else:
                part[first + i] = nt(ya[k], zw[slot])
            return carry

        lax.fori_loop(0, n, one, 0)

    def first_products():
        for c in (1, 2):
            take_y(c, near)
            take_z(c, 0)
        for i, kind in enumerate(("own", "rows", "cols")):
            products(3 * i, 3, kind, 0, lambda i: i + jnp.where(i == 2, 1, 0))
        trade(0).start()

    def last_products():
        for c in (1, 2):
            take_y(c, far)
            take_z(c, 1)
        for i, kind in enumerate(("own", "rows", "cols")):
            products(9 + i, 1, kind, 0, lambda i: 2)
        trade(1).start()

        @pl.when(even)
        def _():
            products(12, 4, "rows", 1, lambda i: i)
            products(16, 4, "cols", 1, lambda i: i)
            trade(2).start()

    def fspread(g, k):
        first, n = GROUPS[g]
        at = pl.ds(pl.multiple_of(arc * half + ((x + k) % 4) * piece, 16), piece)
        return remote(part.at[pl.ds(first, n), at, pl.ds(0, 128)], xf.at[k - 1, pl.ds(first, n)],
                      fxs.at[k, g], fxr.at[k, g], xpeer(k))

    def bspread(g, k):
        first, n = GROUPS[g]
        at = pl.ds(pl.multiple_of(((x + k) % 4) * piece, 16), piece)
        return remote(narrow.at[pl.ds(first, n), at], xb.at[k - 1, pl.ds(first, n)],
                      bxs.at[k, g], bxr.at[k, g], xpeer(k))

    def halves(g):
        first, n = GROUPS[g]
        trade(g).wait()
        rows = pl.ds(pl.multiple_of(arc * half, half), half)

        def add(b, carry):
            both = part[first + b, rows] + dbuf[first + b]
            part[first + b, rows] = both
            narrow[first + b] = both[:, 128:].astype(BF16)
            return carry

        lax.fori_loop(0, n, add, 0)
        for k in turns:
            fspread(g, k).start()

    def spread_rest(g):
        for k in turns:
            bspread(g, k).start()

    lanes = (pl.ds(0, 128), pl.ds(128, size - 128))

    def final(b, w, act):
        target, upper, here = owner(blocks[b])
        src = part.at[b, pl.ds(pl.multiple_of(arc * half + x * piece, 16), piece), lanes[w]]
        dst = fbuf.at[upper, zh, x, :, lanes[w]]
        sem = frecv.at[w, upper, zh, x]

        @pl.when(here)
        def _():
            if act == "start":
                pltpu.make_async_copy(src, dst, sem).start()

        @pl.when(jnp.logical_not(here))
        def _():
            c = remote(src, dst, fsend.at[w, b], sem, target)
            if act == "start":
                c.start()
            else:
                c.wait_send()

    def deliver(g, w):
        first, n = GROUPS[g]
        rows = pl.ds(pl.multiple_of(arc * half + x * piece, 16), piece)
        spread, landed = (fspread, xf) if w == 0 else (bspread, xb)
        for k in turns:
            spread(g, k).wait()

        def add(b, carry):
            at = first + b
            part[at, rows, lanes[w]] = ((part[at, rows, lanes[w]] + landed[0, at].astype(F32))
                                      + (landed[1, at].astype(F32) + landed[2, at].astype(F32)))
            return carry

        lax.fori_loop(0, n, add, 0)
        for b in range(first, first + n):
            final(b, w, "start")

    def both(f, *rest):
        f(1, *rest)

        @pl.when(even)
        def _():
            f(2, *rest)

    prior_row = jnp.concatenate([prior_ref[k] for k in range(6)], axis=1)

    def collect(w):
        width = lanes[w].size
        lane = lax.broadcasted_iota(jnp.int32, (piece, width), 1) + lanes[w].start
        sub = lax.broadcasted_iota(jnp.int32, (piece, width), 0)
        for upper in range(2):
            for xx in range(4):
                for zz in range(2):
                    pltpu.make_async_copy(part.at[0, pl.ds(0, piece), lanes[w]], fbuf.at[upper, zz, xx, :, lanes[w]],
                                          frecv.at[w, upper, zz, xx]).wait()
                first = arc * half + xx * piece
                at = pl.ds(pl.multiple_of(first, 16), piece)
                hit = (lane == sub + first) & (col == row + 8 * upper)
                out_ref[upper, at, lanes[w]] = ((fbuf[upper, 0, xx, :, lanes[w]] + fbuf[upper, 1, xx, :, lanes[w]])
                                                + jnp.where(hit, prior_row[:, lanes[w].start : lanes[w].start + width], 0.0))

    def swap_out(w):
        view = out_ref.at[:, pl.ds(pl.multiple_of(arc * half, half), half), lanes[w]]
        return remote(view, view, osend.at[w], orecv.at[w], mate)

    lead = gt.at[arc, col]
    gz = [remote(lead, lead, gzs.at[k], gzr.at[k], lpeer(k)) for k in turns]
    view = gt.at[arc, pl.ds(y * 4, 4)]
    gy = [remote(view, view, gys.at[k], gyr.at[k], ypeer(k)) for k in turns]
    gc = remote(gt.at[arc], gt.at[arc], gcs, gcr, mate)

    first_products()
    for c in s6:
        c.wait()
    s7.start()
    halves(0)
    spread_rest(0)
    s7.wait()
    hosts = {0: (0, 1, 3), 1: (1, 3), 2: (2, 0, 1), 3: (3, 2)}

    def assemble(t, carry):
        a, yy = t // 4, t % 4
        for z1 in range(4):
            at = pl.ds(pl.multiple_of(yy * 256 + z1 * 64 + a * 32, 32), 32)
            for pair in range(2):
                sides = []
                for z2 in (2 * pair, 2 * pair + 1):
                    sides.append(seen[a, yy, z2, hosts[z2].index(z1)] if z1 in hosts[z2] else jnp.zeros((32, 256), F32))
                for y2 in range(4):
                    cut = slice(y2 * 64, y2 * 64 + 64)
                    v[at, y2 * 256 + pair * 128 : y2 * 256 + pair * 128 + 128] = jnp.concatenate(
                        [sides[0][:, cut], sides[1][:, cut]], axis=1)
        return carry

    lax.fori_loop(0, 8, assemble, 0)

    def symmetric(i, carry):
        at = pl.ds(pl.multiple_of(i * 128, 128), 128)

        def one(j, carry):
            here = pl.ds(pl.multiple_of(j * 128, 128), 128)
            whole = v[at, here] + v[here, at].T
            v[at, here] = whole
            v[here, at] = whole.T
            return carry

        return lax.fori_loop(i, 8, one, carry)

    lax.fori_loop(0, 8, symmetric, 0)

    def split(m):
        first = m.astype(BF16)
        rest = m - first.astype(F32)
        second = rest.astype(BF16)
        return first, second, (rest - second.astype(F32)).astype(BF16)

    def left_parts(m):
        a, b, c = split(m)
        return jnp.concatenate([a, b, a, b, a, c], axis=1)

    def right_parts(m):
        a, b, c = split(m)
        for i, q in enumerate((a, b, b, a, c, a)):
            rcat[i * 128 : i * 128 + 128, :] = q

    def step(p, carry):
        @pl.when(p == 1)
        def _():
            last_products()

        @pl.when(p == 2)
        def _():
            deliver(0, 0)
            deliver(0, 1)

        @pl.when(p == 4)
        def _():
            both(deliver, 0)

        @pl.when(p == 6)
        def _():
            collect(0)
            rows = pl.ds(pl.multiple_of(arc * half, half), half)
            for upper in range(2):
                gt[arc, col, :, upper * half : upper * half + half] = out_ref[upper, rows, 0:128].T[0:64, :]
            for c in gz:
                c.start()
            swap_out(0).start()

        @pl.when(p == 7)
        def _():
            both(deliver, 1)

        b = 128
        at = pl.ds(pl.multiple_of(p * b, b), b)
        inv = factor_inverse(v[at, at])

        @pl.when(p == 1)
        def _():
            both(halves)
            both(spread_rest)

        v[at, at] = jnp.eye(b, dtype=F32)
        right_parts(v[at, :])
        whole = jnp.dot(left_parts(inv), rcat[...], preferred_element_type=F32)
        v[at, :] = whole
        right_parts(whole)

        def below(i, carry):
            here = pl.ds(pl.multiple_of(i * b, b), b)
            left = left_parts(v[at, here].T)
            v[here, at] = jnp.zeros((b, b), F32)
            v[here, :] = v[here, :] - jnp.dot(left, rcat[...], preferred_element_type=F32)
            return carry

        lax.fori_loop(p + 1, 8, below, 0)
        return carry

    lax.fori_loop(0, 8, step, 0)
    for j in range(4):
        v[j * 256 : j * 256 + 128, j * 256 + 128 : j * 256 + 256] = jnp.zeros((128, 128), F32)

    for c in gz:
        c.wait()
    for c in gy:
        c.start()
    collect(1)
    swap_out(1).start()
    for c in gy:
        c.wait()
    gc.start()
    for w in range(2):
        swap_out(w).wait()
    for upper in range(2):
        for kr in range(6):
            for kc in range(6):
                norm_ref[pl.ds((2 * kr + upper) * 384 + kc, 64, stride=6), :] = out_ref[
                    upper, kr * 64 : kr * 64 + 64, kc * 64 : kc * 64 + 64]
    gc.wait()

    def panel(j, carry):
        at = pl.ds(pl.multiple_of(j * 256, 256), 256)

        def one(k, carry):
            here = pl.ds(pl.multiple_of(k * 256, 256), 256)
            return tuple(carry[a] + jnp.dot(v[at, here], gt[a, pl.ds(k * 4, 4)].reshape(256, size),
                                            precision=HIGHEST, preferred_element_type=F32) for a in range(2))

        both = lax.fori_loop(0, j + 1, one, (jnp.zeros((256, size), F32),) * 2)
        for a in range(2):
            turned = both[a].T
            for upper in range(2):
                for kc in range(3):
                    tile = 2 * (a * 3 + kc) + upper
                    panel_ref[tile * 64 : tile * 64 + 64, at] = turned[upper * half + kc * 64 : upper * half + kc * 64 + 64]
        return carry

    lax.fori_loop(0, 4, panel, 0)

    for c in range(len(CHUNKS)):
        zcopy(c, 0).wait_send()

        @pl.when(odd)
        def _():
            zcopy(c, 1).wait_send()

        for k in turns:
            ycopy(c, k).wait_send()
    for w in range(2):
        for b in range(12):
            final(b, w, "end")

        @pl.when(even)
        def _():
            for b in range(12, 20):
                final(b, w, "end")


def normal_and_panel(at, weight, prior):
    size, obs = at.shape
    dma = pltpu.SemaphoreType.DMA
    n = len(CHUNKS)
    return pl.pallas_call(
        kernel,
        out_shape=(jax.ShapeDtypeStruct((12 * size, 64), F32), jax.ShapeDtypeStruct((2 * size, 1024), F32)),
        in_specs=[VMEM] * 3,
        out_specs=(VMEM, VMEM),
        scratch_shapes=[
            pltpu.VMEM((2, size, size), F32),
            pltpu.VMEM((4, size, obs), BF16),
            pltpu.VMEM((2, size, obs), BF16),
            pltpu.VMEM((4, size, obs), BF16),
            pltpu.VMEM((2, size, obs), BF16),
            pltpu.VMEM((20, size, size), F32),
            pltpu.VMEM((20, size // 2, size), F32),
            pltpu.VMEM((20, size // 2, size - 128), BF16),
            pltpu.VMEM((3, 20, size // 8, 128), F32),
            pltpu.VMEM((3, 20, size // 8, size - 128), BF16),
            pltpu.VMEM((2, 2, 4, size // 8, size), F32),
            pltpu.VMEM((3, 64, 256), F32),
            pltpu.VMEM((3, 32, 256), F32),
            pltpu.VMEM((3, 32, 256), F32),
            pltpu.VMEM((4, 3, 8, 256), F32),
            pltpu.VMEM((2, 3, 8, 256), F32),
            pltpu.VMEM((2, 4, 4, 3, 32, 256), F32),
            pltpu.VMEM((1024, 1024), F32),
            pltpu.VMEM((768, 1024), BF16),
            pltpu.VMEM((2, 16, 64, size), F32),
            dma((n, 4)), dma((n, 4)), dma((n, 2)), dma((n, 2)), dma((3,)), dma((3,)),
            dma((4, 3)), dma((4, 3)), dma((4, 3)), dma((4, 3)), dma((2, 20)), dma((2, 2, 2, 4)), dma((2,)), dma((2,)),
            dma, dma, dma((4,)), dma((4,)), dma, dma, dma((4,)), dma((4,)), dma((2, 4)), dma((2, 4)), dma((2, 4)), dma((2, 4)), dma, dma,
            dma((4,)), dma((4,)), dma((4,)), dma((4,)), dma, dma,
        ],
        compiler_params=pltpu.CompilerParams(collective_id=0, has_side_effects=True, vmem_limit_bytes=60 << 20),
        name="normal_and_panel",
    )(at, weight, prior)


def body(design, obs_weight, prior):
    rows_dev, kc_tiles, single, tile = design.shape
    local_cols = kc_tiles * tile
    normal, panel = normal_and_panel(
        design.transpose(1, 2, 3, 0).reshape(local_cols, rows_dev), obs_weight.reshape(1, rows_dev), prior)
    shape = (2 * kc_tiles, 1, tile, kc_tiles, 1, tile)
    return (normal.reshape(shape), panel.reshape(2 * kc_tiles, 1, tile, 1024))


def solution(mesh):
    placed = (P(("arc", "row"), None, "col", None), P(("arc", "row")), P(None, "col", None))
    return jax.shard_map(
        body,
        mesh=mesh,
        in_specs=placed,
        out_specs=(P(None, "row", None, None, "col", None), P(None, "row", None, None)),
        check_vma=False,
    )
```

time: 1250 us -> 213 us (0.17)
  the two profiles are of different devices: /device:TPU:105 before, /device:TPU:131 now
where the time goes in v2:
time: 213 us
  Pallas kernels  204 us (96%)
  local copies, waits for them, and re-layouts  7.87 us (4%)
    pallas_call x1, Pallas kernels, normal_and_panel(): pl.pallas_call(kernel, out_shape=(jax.ShapeDtypeStruct((12 * size, 64), F...  204 us
    unnamed x4, local copies, waits for them, and re-layouts  6.57 us

profile of v2, /device:TPU:131, one launch (start us, length us, event | category | flops | bytes accessed | tf_op | source)
XLA Modules:
  0.0 212.9 jit_solution(10026809732992024079)
XLA Ops:
  0.6 1.3 reshape.17.w_ref
  1.9 204.4 %normal_and_panel.1 = (f32[4608,64]{1,0:T(8,128)}, f32[768,1024]{1,0:T(8,128)}) custom-call(bf16[384,1536]{1,0:T(8,128)(2,1)} %bitcast.9, f32[1,1536]{1,0:T(1,128)} %reshape.17.w_ref, f32[6,1,64]{2,1,0:T(1,128)} %prior_ref.1), custom_call_target="tpu_custom_call" | custom-call | tf_op jit(solution)/shard_map/normal_and_panel/pallas_call | solution.py:587
  206.4 0.0 copy-start
  206.4 4.9 %copy.11 = f32[12,1,64,6,1,64]{5,4,3,2,1,0:T(1,128)} copy(f32[12,1,64,6,1,64]{5,4,3,2,1,0:T(1,128)} %bitcast.8) | data formatting | bytes 2359296
  211.3 0.0 copy-done
  211.3 1.7 copy.12
Async XLA Ops:
  206.4 4.9 %copy-start = (f32[768,1024]{1,0:T(8,128)S(1)}, f32[768,1024]{1,0:T(8,128)}, u32[]{:S(2)}) copy-start(f32[768,1024]{1,0:T(8,128)} %get-tuple-element.5) | copy-start | bytes 9437188

commit v3 on v2

--- a/solution.py
+++ b/solution.py
@@ -69,7 +69,7 @@
     return jnp.where(lane_all <= sub_all, jnp.concatenate(groups, axis=0), 0.0)
 
 
-CHUNKS = ((0, 64), (64, 160), (224, 160))
+CHUNKS = ((0, 64), (64, 128), (192, 192))
 GROUPS = ((0, 9), (9, 3), (12, 8))
 
 
@@ -201,8 +201,6 @@
     take_y(0, far)
     send_z(1, 0)
     send_y(1, near)
-    send_z(2, 0)
-    send_y(2, near)
     ahead_w = yw[:, 0:64, :].reshape(256, obs)
     strip[0] = 0.5 * nt(at_ref[0:64, :], ahead_w)
     ahead_a = ya[:, 0:64, :].reshape(256, obs)
@@ -233,6 +231,7 @@
     for c in s2:
         c.wait()
     sz[zh] = (sx[0] + sx[1]) + (sx[2] + sx[3])
+    send_y(2, near)
     s3 = remote(sz.at[zh], sz.at[zh], s3s, s3r, zpeer)
     s3.start()
     s3.wait()
@@ -259,14 +258,15 @@
     s5 = both_ways(seen.at[arc, y, low, :, own], seen.at[arc, y, high, :, own], s5s, s5r)
     for c in s5:
         c.start()
+    send_z(2, 0)
     for c in s5:
         c.wait()
     s6 = both_ways(seen.at[arc, :, high, :, own], seen.at[arc, y, low], s6s, s6r)
     for c in s6:
         c.start()
     send_z(1, 1)
+    send_z(2, 1)
     send_y(1, far)
-    send_z(2, 1)
     send_y(2, far)
     s7 = remote(seen.at[arc], seen.at[arc], s7s, s7r, mate)
 
@@ -470,18 +470,16 @@
     def step(p, carry):
         @pl.when(p == 1)
         def _():
+            deliver(0, 0)
             last_products()
 
-        @pl.when(p == 2)
-        def _():
-            deliver(0, 0)
+        @pl.when(p == 3)
+        def _():
+            both(deliver, 0)
+            both(spread_rest)
             deliver(0, 1)
 
         @pl.when(p == 4)
-        def _():
-            both(deliver, 0)
-
-        @pl.when(p == 6)
         def _():
             collect(0)
             rows = pl.ds(pl.multiple_of(arc * half, half), half)
@@ -491,8 +489,12 @@
                 c.start()
             swap_out(0).start()
 
-        @pl.when(p == 7)
-        def _():
+        @pl.when(p == 5)
+        def _():
+            for c in gz:
+                c.wait()
+            for c in gy:
+                c.start()
             both(deliver, 1)
 
         b = 128
@@ -502,7 +504,6 @@
         @pl.when(p == 1)
         def _():
             both(halves)
-            both(spread_rest)
 
         v[at, at] = jnp.eye(b, dtype=F32)
         right_parts(v[at, :])
@@ -524,10 +525,6 @@
     for j in range(4):
         v[j * 256 : j * 256 + 128, j * 256 + 128 : j * 256 + 256] = jnp.zeros((128, 128), F32)
 
-    for c in gz:
-        c.wait()
-    for c in gy:
-        c.start()
     collect(1)
     swap_out(1).start()
     for c in gy:
@@ -542,21 +539,33 @@
                     upper, kr * 64 : kr * 64 + 64, kc * 64 : kc * 64 + 64]
     gc.wait()
 
-    def panel(j, carry):
-        at = pl.ds(pl.multiple_of(j * 256, 256), 256)
-
-        def one(k, carry):
-            here = pl.ds(pl.multiple_of(k * 256, 256), 256)
-            return tuple(carry[a] + jnp.dot(v[at, here], gt[a, pl.ds(k * 4, 4)].reshape(256, size),
-                                            precision=HIGHEST, preferred_element_type=F32) for a in range(2))
-
-        both = lax.fori_loop(0, j + 1, one, (jnp.zeros((256, size), F32),) * 2)
+    def panel(k, carry):
         for a in range(2):
-            turned = both[a].T
-            for upper in range(2):
-                for kc in range(3):
-                    tile = 2 * (a * 3 + kc) + upper
-                    panel_ref[tile * 64 : tile * 64 + 64, at] = turned[upper * half + kc * 64 : upper * half + kc * 64 + 64]
+            pieces = split(gt[a, pl.ds(k * 4, 4)].reshape(256, size))
+            for u in range(12):
+                q = (0, 1, 1, 0, 2, 0)[u // 2]
+                yw[u // 3, (u % 3) * 128 : (u % 3) * 128 + 128, a * size : a * size + size] = (
+                    pieces[q][(u % 2) * 128 : (u % 2) * 128 + 128])
+
+        def one(j, carry):
+            left = left_parts(v[pl.ds(pl.multiple_of(j * 256, 256), 256), pl.ds(pl.multiple_of(k * 256, 256), 256)])
+            got = jnp.dot(left, yw[:, :, 0 : 2 * size].reshape(1536, 2 * size), preferred_element_type=F32)
+            for a in range(2):
+                for h in range(2):
+                    at = j * 4 + a * 2 + h
+                    new = got[h * 128 : h * 128 + 128, a * size : a * size + size]
+                    dbuf[at, 0:128] = jnp.where(k == 0, new, dbuf[at, 0:128] + new)
+            return carry
+
+        lax.fori_loop(k, 4, one, 0)
+        for a in range(2):
+            for h in range(2):
+                turned = dbuf[k * 4 + a * 2 + h, 0:128].T
+                at = pl.ds(pl.multiple_of(k * 256 + h * 128, 128), 128)
+                for upper in range(2):
+                    for kc in range(3):
+                        tile = 2 * (a * 3 + kc) + upper
+                        panel_ref[tile * 64 : tile * 64 + 64, at] = turned[upper * half + kc * 64 : upper * half + kc * 64 + 64]
         return carry
 
     lax.fori_loop(0, 4, panel, 0)

time: 213 us -> 194 us (0.911)
  the two profiles are of different devices: /device:TPU:131 before, /device:TPU:95 now
where the time goes in v3:
time: 194 us
  Pallas kernels  185 us (95%)
  local copies, waits for them, and re-layouts  7.87 us (4%)
    pallas_call x1, Pallas kernels, normal_and_panel(): pl.pallas_call(kernel, out_shape=(jax.ShapeDtypeStruct((12 * size, 64), F...  185 us
    unnamed x4, local copies, waits for them, and re-layouts  6.57 us

profile of v3, /device:TPU:95, one launch (start us, length us, event | category | flops | bytes accessed | tf_op | source)
XLA Modules:
  0.0 193.5 jit_solution(6701464646950592343)
XLA Ops:
  0.6 1.3 reshape.17.w_ref
  1.9 185.0 %normal_and_panel.1 = (f32[4608,64]{1,0:T(8,128)}, f32[768,1024]{1,0:T(8,128)}) custom-call(bf16[384,1536]{1,0:T(8,128)(2,1)} %bitcast.9, f32[1,1536]{1,0:T(1,128)} %reshape.17.w_ref, f32[6,1,64]{2,1,0:T(1,128)} %prior_ref.1), custom_call_target="tpu_custom_call" | custom-call | tf_op jit(solution)/shard_map/normal_and_panel/pallas_call | solution.py:596
  187.0 0.0 copy-start
  187.0 4.9 %copy.11 = f32[12,1,64,6,1,64]{5,4,3,2,1,0:T(1,128)} copy(f32[12,1,64,6,1,64]{5,4,3,2,1,0:T(1,128)} %bitcast.8) | data formatting | bytes 2359296
  191.9 0.0 copy-done
  191.9 1.7 copy.12
Async XLA Ops:
  187.0 4.9 %copy-start = (f32[768,1024]{1,0:T(8,128)S(1)}, f32[768,1024]{1,0:T(8,128)}, u32[]{:S(2)}) copy-start(f32[768,1024]{1,0:T(8,128)} %get-tuple-element.5) | copy-start | bytes 9437188

commit v4 on v3

--- a/solution.py
+++ b/solution.py
@@ -407,10 +407,13 @@
         view = out_ref.at[:, pl.ds(pl.multiple_of(arc * half, half), half), lanes[w]]
         return remote(view, view, osend.at[w], orecv.at[w], mate)
 
-    lead = gt.at[arc, col]
-    gz = [remote(lead, lead, gzs.at[k], gzr.at[k], lpeer(k)) for k in turns]
-    view = gt.at[arc, pl.ds(y * 4, 4)]
-    gy = [remote(view, view, gys.at[k], gyr.at[k], ypeer(k)) for k in turns]
+    most, others = pl.ds(0, 40), pl.ds(40, 24)
+    here = (gt.at[arc, y, zl, most], gt.at[arc, y, zl, others])
+    gz = ([remote(here[0], here[0], gzs.at[0, k], gzr.at[0, k], lpeer(k)) for k in turns]
+          + [remote(here[1], here[1], gzs.at[1, k], gzr.at[1, k], ypeer(k)) for k in turns])
+    there = (gt.at[arc, y, :, most], gt.at[arc, :, zl, others])
+    gy = ([remote(there[0], there[0], gys.at[0, k], gyr.at[0, k], ypeer(k)) for k in turns]
+          + [remote(there[1], there[1], gys.at[1, k], gyr.at[1, k], lpeer(k)) for k in turns])
     gc = remote(gt.at[arc], gt.at[arc], gcs, gcr, mate)
 
     first_products()
@@ -473,23 +476,23 @@
             deliver(0, 0)
             last_products()
 
-        @pl.when(p == 3)
+        @pl.when(p == 2)
         def _():
             both(deliver, 0)
             both(spread_rest)
             deliver(0, 1)
 
-        @pl.when(p == 4)
+        @pl.when(p == 3)
         def _():
             collect(0)
             rows = pl.ds(pl.multiple_of(arc * half, half), half)
             for upper in range(2):
-                gt[arc, col, :, upper * half : upper * half + half] = out_ref[upper, rows, 0:128].T[0:64, :]
+                gt[arc, y, zl, :, upper * half : upper * half + half] = out_ref[upper, rows, 0:128].T[0:64, :]
             for c in gz:
                 c.start()
             swap_out(0).start()
 
-        @pl.when(p == 5)
+        @pl.when(p == 4)
         def _():
             for c in gz:
                 c.wait()
@@ -541,7 +544,7 @@
 
     def panel(k, carry):
         for a in range(2):
-            pieces = split(gt[a, pl.ds(k * 4, 4)].reshape(256, size))
+            pieces = split(gt[a, k].reshape(256, size))
             for u in range(12):
                 q = (0, 1, 1, 0, 2, 0)[u // 2]
                 yw[u // 3, (u % 3) * 128 : (u % 3) * 128 + 128, a * size : a * size + size] = (
@@ -618,11 +621,11 @@
             pltpu.VMEM((2, 4, 4, 3, 32, 256), F32),
             pltpu.VMEM((1024, 1024), F32),
             pltpu.VMEM((768, 1024), BF16),
-            pltpu.VMEM((2, 16, 64, size), F32),
+            pltpu.VMEM((2, 4, 4, 64, size), F32),
             dma((n, 4)), dma((n, 4)), dma((n, 2)), dma((n, 2)), dma((3,)), dma((3,)),
             dma((4, 3)), dma((4, 3)), dma((4, 3)), dma((4, 3)), dma((2, 20)), dma((2, 2, 2, 4)), dma((2,)), dma((2,)),
             dma, dma, dma((4,)), dma((4,)), dma, dma, dma((4,)), dma((4,)), dma((2, 4)), dma((2, 4)), dma((2, 4)), dma((2, 4)), dma, dma,
-            dma((4,)), dma((4,)), dma((4,)), dma((4,)), dma, dma,
+            dma((2, 4)), dma((2, 4)), dma((2, 4)), dma((2, 4)), dma, dma,
         ],
         compiler_params=pltpu.CompilerParams(collective_id=0, has_side_effects=True, vmem_limit_bytes=60 << 20),
         name="normal_and_panel",

time: 194 us -> 191 us (0.985)
  the two profiles are of different devices: /device:TPU:95 before, /device:TPU:105 now
where the time goes in v4:
time: 191 us
  Pallas kernels  182 us (95%)
  local copies, waits for them, and re-layouts  7.87 us (4%)
    pallas_call x1, Pallas kernels, normal_and_panel(): pl.pallas_call(kernel, out_shape=(jax.ShapeDtypeStruct((12 * size, 64), F...  182 us
    unnamed x4, local copies, waits for them, and re-layouts  6.57 us

profile of v4, /device:TPU:105, one launch (start us, length us, event | category | flops | bytes accessed | tf_op | source)
XLA Modules:
  0.0 190.5 jit_solution(14359545364311996825)
XLA Ops:
  0.6 1.3 reshape.17.w_ref
  1.9 182.0 %normal_and_panel.1 = (f32[4608,64]{1,0:T(8,128)}, f32[768,1024]{1,0:T(8,128)}) custom-call(bf16[384,1536]{1,0:T(8,128)(2,1)} %bitcast.9, f32[1,1536]{1,0:T(1,128)} %reshape.17.w_ref, f32[6,1,64]{2,1,0:T(1,128)} %prior_ref.1), custom_call_target="tpu_custom_call" | custom-call | tf_op jit(solution)/shard_map/normal_and_panel/pallas_call | solution.py:599
  183.9 0.0 copy-start
  183.9 4.9 %copy.11 = f32[12,1,64,6,1,64]{5,4,3,2,1,0:T(1,128)} copy(f32[12,1,64,6,1,64]{5,4,3,2,1,0:T(1,128)} %bitcast.8) | data formatting | bytes 2359296
  188.8 0.0 copy-done
  188.8 1.7 copy.12
Async XLA Ops:
  183.9 4.9 %copy-start = (f32[768,1024]{1,0:T(8,128)S(1)}, f32[768,1024]{1,0:T(8,128)}, u32[]{:S(2)}) copy-start(f32[768,1024]{1,0:T(8,128)} %get-tuple-element.5) | copy-start | bytes 9437188

commit v5 on v4

--- a/solution.py
+++ b/solution.py
@@ -476,12 +476,6 @@
             deliver(0, 0)
             last_products()
 
-        @pl.when(p == 2)
-        def _():
-            both(deliver, 0)
-            both(spread_rest)
-            deliver(0, 1)
-
         @pl.when(p == 3)
         def _():
             collect(0)
@@ -507,6 +501,12 @@
         @pl.when(p == 1)
         def _():
             both(halves)
+
+        @pl.when(p == 2)
+        def _():
+            both(deliver, 0)
+            both(spread_rest)
+            deliver(0, 1)
 
         v[at, at] = jnp.eye(b, dtype=F32)
         right_parts(v[at, :])

time: 191 us -> 192 us (level)
  no operation moved by 1% of the time
where the time goes in v5:
time: 192 us
  Pallas kernels  183 us (95%)
  local copies, waits for them, and re-layouts  7.87 us (4%)
    pallas_call x1, Pallas kernels, normal_and_panel(): pl.pallas_call(kernel, out_shape=(jax.ShapeDtypeStruct((12 * size, 64), F...  183 us
    unnamed x4, local copies, waits for them, and re-layouts  6.57 us

profile of v5, /device:TPU:105, one launch (start us, length us, event | category | flops | bytes accessed | tf_op | source)
XLA Modules:
  0.0 191.9 jit_solution(17377912320104875346)
XLA Ops:
  0.6 1.3 reshape.17.w_ref
  1.9 183.3 %normal_and_panel.1 = (f32[4608,64]{1,0:T(8,128)}, f32[768,1024]{1,0:T(8,128)}) custom-call(bf16[384,1536]{1,0:T(8,128)(2,1)} %bitcast.9, f32[1,1536]{1,0:T(1,128)} %reshape.17.w_ref, f32[6,1,64]{2,1,0:T(1,128)} %prior_ref.1), custom_call_target="tpu_custom_call" | custom-call | tf_op jit(solution)/shard_map/normal_and_panel/pallas_call | solution.py:599
  185.3 0.0 copy-start
  185.3 4.9 %copy.11 = f32[12,1,64,6,1,64]{5,4,3,2,1,0:T(1,128)} copy(f32[12,1,64,6,1,64]{5,4,3,2,1,0:T(1,128)} %bitcast.8) | data formatting | bytes 2359296
  190.2 0.0 copy-done
  190.2 1.7 copy.12
Async XLA Ops:
  185.3 4.9 %copy-start = (f32[768,1024]{1,0:T(8,128)S(1)}, f32[768,1024]{1,0:T(8,128)}, u32[]{:S(2)}) copy-start(f32[768,1024]{1,0:T(8,128)} %get-tuple-element.5) | copy-start | bytes 9437188
